TPU v7x, 256 devices: a whole 4x4x8 slice. The times are simulated.
256 devices in a mesh: dp: 16 (over x, y_lo, core), head: 16 (over z, y_hi).
Axes of the slice: x: 4, y: 4 (y_hi: 2, y_lo: 2; y = y_hi * 2 + y_lo), z: 8, core: 2. Of those that a mesh axis runs over, the one named last changes fastest.
Arguments:
- queries: bfloat16 [32768, 4096], P('dp', 'head'), may hold values from -12 to 12
- keys: bfloat16 [32768, 2048], P('dp', 'head'), may hold values from -12 to 12
- values: bfloat16 [32768, 2048], P('dp', 'head'), may hold values from -6 to 6
- doc_lengths: int32 [16, 16], replicated, may hold values from 0 to 2048, as said below
- out_weight: bfloat16 [4096, 4608], P(None, 'dp'), may hold values from -0.09375 to 0.09375
Outputs:
- mixed: bfloat16 [16, 2048, 4608], P(None, 'head', 'dp')
Inputs may be any that keep to these rules, and one draw needn't show every extreme that they name: `doc_lengths`: row r holds the lengths of the documents packed into sequence r in order, each a multiple of 128, summing to 2048, followed by zeros; some row holds a single document of 2048 tokens.
All inputs are finite; a program needn't handle non-finite values.
Results may differ from a plain program's by a relative error of at most 0.014.
Values may be sent and summed in bfloat16 or wider, within the bound.
A program may use at most 128 MiB of HBM per device.

v0:
```python
import jax
import jax.numpy as jnp
from jax import lax
from jax.sharding import PartitionSpec as P

HD = 128
BLK = 512


query_scale = 1.0 / 12.0
soft_cap = 50.0


def doc_index(lengths_row, length):
    doc_ends = jnp.cumsum(lengths_row)
    positions = jnp.arange(length, dtype=jnp.int32)
    return jnp.sum((doc_ends[None, :] <= positions[:, None]).astype(jnp.int32), axis=1)


def tile_live(doc_of, row_block, col_block):
    return doc_of[(col_block + 1) * BLK - 1] == doc_of[row_block * BLK]


def attend_block(query_block, key_heads, value_heads, doc_of, row_block):
    kv_heads = key_heads.shape[1]
    group_size = query_block.shape[2]
    q_doc = doc_of[row_block * BLK : (row_block + 1) * BLK]
    q_pos = row_block * BLK + jnp.arange(BLK, dtype=jnp.int32)
    numerator = jnp.zeros((BLK, kv_heads, group_size, HD), jnp.float32)
    denominator = jnp.zeros((BLK, kv_heads, group_size), jnp.float32)
    for col_block in range(row_block + 1):
        key_block = key_heads[col_block * BLK : (col_block + 1) * BLK]
        value_block = value_heads[col_block * BLK : (col_block + 1) * BLK]
        k_doc = doc_of[col_block * BLK : (col_block + 1) * BLK]
        k_pos = col_block * BLK + jnp.arange(BLK, dtype=jnp.int32)

        def add_tile(
            carried, key_block=key_block, value_block=value_block, k_doc=k_doc, k_pos=k_pos
        ):
            raw_score = jnp.einsum(
                "qhgd,phd->hgqp", query_block, key_block, preferred_element_type=jnp.float32
            )
            capped = soft_cap * jnp.tanh(raw_score * query_scale / soft_cap)
            allowed = (q_doc[:, None] == k_doc[None, :]) & (q_pos[:, None] >= k_pos[None, :])
            weight = jnp.where(allowed[None, None], jnp.exp(capped), jnp.float32(0.0)).astype(
                jnp.bfloat16
            )
            part_num = jnp.einsum(
                "hgqp,phd->qhgd", weight, value_block, preferred_element_type=jnp.float32
            )
            part_den = jnp.sum(weight, axis=3, dtype=jnp.float32).transpose(2, 0, 1)
            return (carried[0] + part_num, carried[1] + part_den)

        if col_block == row_block:
            numerator, denominator = add_tile((numerator, denominator))
        else:
            numerator, denominator = lax.cond(
                tile_live(doc_of, row_block, col_block),
                add_tile,
                lambda carried: carried,
                (numerator, denominator),
            )
    result = (numerator / denominator[..., None]).astype(jnp.bfloat16)
    return result.reshape(BLK, kv_heads * group_size * HD)


def body(queries, keys, values, doc_lengths, out_weight):
    length = queries.shape[0]
    kv_heads = keys.shape[1] // HD
    group_size = queries.shape[1] // HD // kv_heads
    blocks = length // BLK
    query_heads = queries.reshape(length, kv_heads, group_size, HD)
    key_heads = keys.reshape(length, kv_heads, HD)
    value_heads = values.reshape(length, kv_heads, HD)
    replica = lax.axis_index("dp")
    own_lengths = lax.dynamic_slice_in_dim(doc_lengths, replica, 1, 0)[0]
    own_docs = doc_index(own_lengths, length)
    outputs = [
        attend_block(
            query_heads[row_block * BLK : (row_block + 1) * BLK],
            key_heads,
            value_heads,
            own_docs,
            row_block,
        )
        for row_block in range(blocks)
    ]
    attended = jnp.concatenate(outputs, axis=0)
    head_count = lax.axis_size("head")
    part_rows = length // head_count
    features = attended.shape[1]
    regrouped = lax.all_to_all(
        attended.reshape(head_count, part_rows, features),
        "head",
        split_axis=0,
        concat_axis=2,
        tiled=True,
    )
    regrouped = regrouped.reshape(part_rows, head_count * features)
    mixed = jnp.dot(
        lax.all_gather(regrouped, "dp", axis=0, tiled=True),
        out_weight,
        preferred_element_type=jnp.float32,
    ).astype(jnp.bfloat16)
    return mixed.reshape(-1, part_rows, out_weight.shape[1])


def solution(mesh):
    return jax.shard_map(
        body,
        mesh=mesh,
        in_specs=(P("dp", "head"), P("dp", "head"), P("dp", "head"), P(), P(None, "dp")),
        out_specs=P(None, "head", "dp"),
        check_vma=False,
    )
```

profile of v0, /device:TPU:1, one launch (start us, length us, event | category | flops | bytes accessed | tf_op | source)
XLA Modules:
  0.0 233.7 jit_solution(1506058562753663382)
XLA Ops:
  17.0 1.8 fusion.74
  18.7 1.1 fusion.73
  20.9 2.0 fusion.72
  22.8 1.8 copy.187
  26.5 1.8 fusion.52
  28.3 1.9 convert_reduce_fusion.9
  30.2 1.2 fusion.47
  33.0 2.2 compare_and_fusion.7
  35.2 5.6 %conditional.11 = (f32[512,1,2]{0,2,1:T(2,128)}, f32[512,1,2,128]{0,3,2,1:T(8,128)}) conditional(s32[]{:T(128)} %bitcast.124, (f32[512,1,2,128]{3,0,2,1:T(8,128)S(1)}, f32[512,1,2]{0,2,1:T(2,128)}) %get-tuple-element.455, (s32[512]{0:T(512)}, s32[512]{0:T(512)S(1)}, s32[512]{0:T(512)S(1)}, s32[512]{0:T(512)S(1)}, ...), branch_computations={%region_20.21_spmd, %region_21.23_spmd} | conditional | flops 272498688 | bytes 5791788 | solution.py:57
  36.2 1.8 convert_reduce_fusion.5
  38.5 1.3 bitcast_add_fusion.2
  40.7 1.9 convert_reduce_fusion.6
  43.4 1.4 fusion.43
  45.8 3.4 %convert_reduce_fusion.8 = (f32[2,512]{1,0:T(2,128)}, bf16[1,2,512,512]{2,3,1,0:T(8,128)(2,1)}) fusion(bf16[512,2,128]{0,2,1:T(8,128)(2,1)S(1)} %bitcast.410, bf16[2048,128]{1,0:T(8,128)(2,1)} %param.18, pred[512,512]{0,1:T(8,128)(4,1)S(1)} %copy-done.9), kind=kOutput, calls=%fused_computation.70 | convolution fusion | flops 137362432 | bytes 1708032 | tf_op jit(solution)/shard_map/qhgd,phd->hgqp/dot_general | solution.py:40
  49.1 2.4 %conditional.6 = (f32[512,1,2]{0,2,1:T(2,128)}, f32[512,1,2,128]{0,3,2,1:T(8,128)S(1)}) conditional(s32[]{:T(128)} %bitcast.90, () %tuple.47, (s32[512]{0:T(512)S(1)}, s32[512]{0:T(512)S(1)}, s32[512]{0:T(512)S(1)}, s32[512]{0:T(512)S(1)}, bf16[512,1,128]{2,0,1:T(8,128)(2,1)S(1)}, /*index=5*/bf16[512,256]{0,1:T(8,128)(2,1)S(1)}, ...), branch_computations={%region_3.4_spmd, %region_4.6_spmd} | conditional | flops 272366592 | bytes 4730896 | solution.py:57
  49.4 1.4 convert_reduce_fusion
  52.3 1.6 fusion.45
  56.7 1.9 convert_reduce_fusion.7
  59.4 2.1 fusion.44
  62.7 33.0 %all_to_all.15 = bf16[16,128,256]{2,1,0:T(8,128)(2,1)S(1)} all-to-all(bf16[16,128,256]{2,1,0:T(8,128)(2,1)S(1)} %bitcast.400), channel_id=1, replica_groups=mesh['dp'=16,'head'=16] {'head'}, dimensions={0} | all-to-all | bytes 2097152 | tf_op jit(solution)/shard_map/all_to_all | solution.py:92
  95.8 1.3 copy.160
  97.1 119.7 %all-gather.2.cloned.1.call-done = bf16[2048,4096]{0,1:T(8,128)(2,1)} async-done(((bf16[128,4096]{0,1:T(8,128)(2,1)}), bf16[2048,4096]{0,1:T(8,128)(2,1)}) %all-gather.2.cloned.1.call-update) | async-done | bytes 16777232 | tf_op jit(solution)/shard_map/all_gather | solution.py:101
  216.8 8.8 %fusion.36 = bf16[36,16,8,128]{3,2,1,0:T(8,128)(2,1)S(1)} fusion(bf16[4096,288]{0,1:T(8,128)(2,1)S(1)} %copy-done, bf16[2048,4096]{0,1:T(8,128)(2,1)} %all-gather.2.cloned.1.call-done), kind=kOutput, calls=%fused_computation.72 | convolution fusion | flops 4832428032 | bytes 20316160 | tf_op jit(solution)/shard_map/dot_general | solution.py:100
  225.6 1.2 copy.196
  (72 shorter events, 19.4 us)
Async XLA Ops:
  6.5 210.3 %copy-start = (bf16[4096,288]{0,1:T(8,128)(2,1)S(1)}, bf16[4096,288]{0,1:T(8,128)(2,1)}, u32[]{:S(2)}) copy-start(bf16[4096,288]{0,1:T(8,128)(2,1)} %param.21) | copy-start | bytes 7077892
  6.5 210.3 %all-gather.2.cloned.1.call-start = ((), (), s32[]{:S(2)}) async-start(), calls=%async_computation.1 | async-start | bytes 17825792 | tf_op jit(solution)/shard_map/all_gather | solution.py:101
  18.7 16.4 %copy-start.10 = (bf16[512,1,128]{2,0,1:T(8,128)(2,1)}, bf16[512,1,128]{2,0,1:T(8,128)(2,1)S(1)}, u32[]{:S(2)}) copy-start(bf16[512,1,128]{2,0,1:T(8,128)(2,1)S(1)} %get-tuple-element.408) | copy-start | bytes 393220
  20.7 14.4 %copy-start.1 = (bf16[512,128]{0,1:T(8,128)(2,1)}, bf16[512,128]{0,1:T(8,128)(2,1)S(1)}, u32[]{:S(2)}) copy-start(bf16[512,128]{0,1:T(8,128)(2,1)S(1)} %copy.189) | copy-start | bytes 393220
  26.5 8.7 %copy-start.8 = (bf16[512,256]{0,1:T(8,128)(2,1)}, bf16[512,256]{0,1:T(8,128)(2,1)S(1)}, u32[]{:S(2)}) copy-start(bf16[512,256]{0,1:T(8,128)(2,1)S(1)} %copy.192) | copy-start | bytes 786436
  36.1 1.8 copy-start.6
  42.7 3.1 %copy-start.7 = (bf16[512,256]{0,1:T(8,128)(2,1)S(1)}, bf16[512,256]{0,1:T(8,128)(2,1)}, u32[]{:S(2)}) copy-start(bf16[512,256]{0,1:T(8,128)(2,1)} %copy.188) | copy-start | bytes 786436
  42.7 3.1 %copy-start.9 = (pred[512,512]{0,1:T(8,128)(4,1)S(1)}, pred[512,512]{0,1:T(8,128)(4,1)}, u32[]{:S(2)}) copy-start(pred[512,512]{0,1:T(8,128)(4,1)} %get-tuple-element.430) | copy-start | bytes 786436
  45.7 3.4 %copy-start.12 = (bf16[512,1,128]{2,0,1:T(8,128)(2,1)S(1)}, bf16[512,1,128]{2,0,1:T(8,128)(2,1)}, u32[]{:S(2)}) copy-start(bf16[512,1,128]{2,0,1:T(8,128)(2,1)} %get-tuple-element.407) | copy-start | bytes 393220
  45.8 3.4 %copy-start.13 = (s32[512]{0:T(512)S(1)}, s32[512]{0:T(512)}, u32[]{:S(2)}) copy-start(s32[512]{0:T(512)} %get-tuple-element.417) | copy-start | bytes 6148
  45.8 3.4 %copy-start.14 = (s32[512]{0:T(512)S(1)}, s32[512]{0:T(512)}, u32[]{:S(2)}) copy-start(s32[512]{0:T(512)} %get-tuple-element.418) | copy-start | bytes 6148
  54.8 0.9 copy-start.11
  58.6 4.0 %copy-start.3 = (bf16[512,256]{1,0:T(8,128)(2,1)S(1)}, bf16[512,256]{1,0:T(8,128)(2,1)}, u32[]{:S(2)}) copy-start(bf16[512,256]{1,0:T(8,128)(2,1)} %copy.156) | copy-start | bytes 786436
  58.6 4.0 %copy-start.4 = (bf16[512,256]{1,0:T(8,128)(2,1)S(1)}, bf16[512,256]{1,0:T(8,128)(2,1)}, u32[]{:S(2)}) copy-start(bf16[512,256]{1,0:T(8,128)(2,1)} %copy.159) | copy-start | bytes 786436
  58.6 4.0 %copy-start.5 = (bf16[512,256]{1,0:T(8,128)(2,1)S(1)}, bf16[512,256]{1,0:T(8,128)(2,1)}, u32[]{:S(2)}) copy-start(bf16[512,256]{1,0:T(8,128)(2,1)} %copy.157) | copy-start | bytes 786436
Sparse Core Ops, SparseCore 0:
  97.2 119.5 all-gather.1
where the time goes:
time: 234 us
  waiting for transfers between devices  120 us (51%)
  blocking collectives  33 us (14%)
  matrix products  28.6 us (12%)
  local copies, waits for them, and re-layouts  21.6 us (9%)
  between operations  21.6 us (9%)
  other arithmetic  9.03 us (4%)
    all_gather x1, waiting for transfers between devices, body(): lax.all_gather(regrouped, 'dp', axis=0, tiled=True)  120 us
    all_to_all x1, blocking collectives, body(): lax.all_to_all(attended.reshape(head_count, part_rows, features), 'head',...  33 us
    dot_general x6, matrix products, add_tile(): jnp.einsum('qhgd,phd->hgqp', query_block, key_block, preferred_element_ty...  12.4 us
    dot_general x1, matrix products, body(): jnp.dot(lax.all_gather(regrouped, 'dp', axis=0, tiled=True), out_weight,...  8.78 us
    dot_general x6, matrix products, add_tile(): jnp.einsum('hgqp,phd->qhgd', weight, value_block, preferred_element_type=...  7.4 us
    and x4, other arithmetic, add_tile(): (q_doc[:, None] == k_doc[None, :]) & (q_pos[:, None] >= k_pos[None, :])  5.23 us
    unnamed x33, local copies, waits for them, and re-layouts  4.95 us
  transfers between devices with their start and end apart: 1, of which 1 were waited for; matrix products, arithmetic and copies ran while one was open for 0% of the time, Pallas kernels for 0%

commit v1 on v0

v1 whole, which is shorter than its diff:
```python
import math

import jax
import jax.numpy as jnp
from jax import lax
from jax.experimental import pallas as pl
from jax.experimental.pallas import tpu as pltpu
from jax.sharding import PartitionSpec as P

HD = 128
BLK = 128
SEQ = 2048
STEPS = 8
CHUNK = 256
FEAT = 288
MAIN = 256
REM = FEAT - MAIN
HEADS = 16
DEPTH = 4096
OROWS = BLK + 16
SCALE = 1.0 / 12.0 / 50.0
GAIN = 50.0 * math.log2(math.e)
MESH = pl.DeviceIdType.MESH
F32 = jnp.float32
BF16 = jnp.bfloat16


def lane_group(rows):
    return lax.broadcasted_iota(jnp.int32, (rows, 128), 1) // REM


def merge_lanes(parts, group):
    out = parts[0]
    for g in range(1, 4):
        out = jnp.where(group == g, parts[g], out)
    return out


def roll(x, by):
    by = by % 128
    return x if by == 0 else pltpu.roll(x, by, 1)


def kernel(
    q_hbm, k_hbm, v_hbm, doc_ref, w_hbm, out_ref,
    q_ref, k_ref, v_ref, w_ref, block_doc,
    acc, stage, gathered, wm, pk, rem_w, acc1, acc2, ostage, obuf,
    ld_sem, a_send, a_recv, x_send, x_recv, f_send, f_recv,
    w_send, w_recv, p_send, p_recv, s_send, s_recv, o_send, o_recv,
):
    dp, head = lax.axis_index("dp"), lax.axis_index("head")
    x, low = dp // 4, lax.rem(dp, 4)
    right = lax.rem(x + 1, 4) * 4 + low
    left = lax.rem(x + 3, 4) * 4 + low
    core_mate = dp + 1 - 2 * lax.rem(dp, 2)
    y_mate = dp + 2 - 4 * lax.rem(dp // 2, 2)
    both_mate = core_mate + 2 - 4 * lax.rem(dp // 2, 2)
    head_mate = head + 1 - 2 * lax.rem(head, 2)
    half = head // 8
    pair = jnp.minimum(head, 15 - head)
    mates = (dp, core_mate, y_mate, both_mate)

    def copy_to(src, dst, send, recv, to_dp, to_head):
        return pltpu.make_async_remote_copy(
            src_ref=src, dst_ref=dst, send_sem=send, recv_sem=recv,
            device_id={"dp": to_dp, "head": to_head}, device_id_type=MESH,
        )

    loads = [
        pltpu.make_async_copy(q_hbm, q_ref, ld_sem.at[0]),
        pltpu.make_async_copy(k_hbm, k_ref, ld_sem.at[1]),
        pltpu.make_async_copy(v_hbm, v_ref, ld_sem.at[2]),
        pltpu.make_async_copy(w_hbm, w_ref, ld_sem.at[3]),
    ]
    for load in loads:
        load.start()
    barrier = pltpu.get_barrier_semaphore()

    def greet(d, to_dp, to_head):
        pl.semaphore_signal(barrier, inc=1, device_id={"dp": to_dp, "head": to_head}, device_id_type=MESH)

    def greet_heads(n, _):
        greet(None, dp, lax.rem(head + n, HEADS))
        return 0

    lax.fori_loop(1, HEADS, greet_heads, 0)
    greet(None, right, head)
    greet(None, left, head)
    greet(None, core_mate, head)
    greet(None, y_mate, head)
    greet(None, both_mate, head)
    greet(None, y_mate, head_mate)

    ends = []
    total = jnp.int32(0)
    for n in range(16):
        total = total + doc_ref[dp, n]
        ends.append(total)

    def number(b, _):
        count = jnp.int32(0)
        for end in ends:
            count = count + jnp.where(end <= b * BLK, 1, 0).astype(jnp.int32)
        block_doc[b] = count
        return 0

    lax.fori_loop(0, 16, number, 0)
    for load in loads[:3]:
        load.wait()
    pl.semaphore_wait(barrier, 21)

    def w_copy(way, n):
        rows = pl.ds(pl.multiple_of(way * 2048 + n * 256, 256), 256)
        return copy_to(
            w_hbm.at[rows, pl.ds(0, MAIN)], wm.at[1, rows], w_send.at[way, n], w_recv.at[way, n],
            y_mate, head if way == 0 else head_mate,
        )

    def p_copy(way):
        rows = pl.ds(way * 512, 512)
        return copy_to(
            pk.at[0, rows], pk.at[2, rows], p_send.at[way], p_recv.at[way],
            y_mate, head if way == 0 else head_mate,
        )

    def core_copy(n):
        if n == 0:
            src, dst = w_hbm.at[:, pl.ds(0, MAIN)], wm.at[0]
        elif n == 1:
            src, dst = pk.at[0], pk.at[1]
        elif n == 2:
            src, dst = wm.at[1], wm.at[2]
        else:
            src, dst = pk.at[2], pk.at[3]
        return copy_to(src, dst, s_send.at[n], s_recv.at[n], core_mate, head)

    def a_copy(t, s, to_head):
        return copy_to(stage.at[t, s], gathered.at[0, t, half], a_send.at[t, s], a_recv.at[t, half], dp, to_head)

    def a_arrival(u, s):
        return copy_to(stage.at[u, s], gathered.at[0, u, s], a_send.at[u, s], a_recv.at[u, s], dp, head)

    def x_copy(way, u):
        return copy_to(
            gathered.at[0, u], gathered.at[1 + way, u], x_send.at[way, u], x_recv.at[way, u],
            right if way == 0 else left, head,
        )

    def f_copy(way, u):
        return copy_to(
            gathered.at[1 + way, u, way], gathered.at[3, u, way], f_send.at[way, u], f_recv.at[way, u],
            right if way == 0 else left, head,
        )

    differences = lax.rem(lax.broadcasted_iota(jnp.int32, (2 * BLK, CHUNK), 0), BLK) - lax.broadcasted_iota(
        jnp.int32, (2 * BLK, CHUNK), 1
    )

    def tile(block, chunk, diagonal):
        rows = pl.ds(pl.multiple_of(block * BLK, BLK), BLK)
        cols = pl.ds(pl.multiple_of(chunk * CHUNK, CHUNK), CHUNK)
        q_two = jnp.concatenate([q_ref[rows, 0:HD], q_ref[rows, HD : 2 * HD]], axis=0)
        raw = lax.dot_general(q_two, k_ref[cols, :], (((1,), (1,)), ((), ())), preferred_element_type=F32)
        weight = jnp.exp2(jnp.tanh(raw * SCALE) * GAIN)
        if diagonal:
            weight = jnp.where(differences >= chunk * CHUNK - block * BLK, weight, 0.0)
        own = block_doc[block]
        live = [
            jnp.full((BLK, HD), jnp.where(block_doc[2 * chunk + n] == own, 1.0, 0.0).astype(F32), F32).astype(BF16)
            for n in range(2)
        ]
        live = jnp.concatenate(live, axis=0)
        value_two = jnp.concatenate([v_ref[cols, :] * live, live], axis=1)
        return jnp.dot(weight.astype(BF16), value_two, preferred_element_type=F32)

    def attend(t):
        j = lax.rem(head + t, 8)
        first = jnp.where(half == 0, j, 15 - j)
        second = 15 - first
        near = first // 2
        acc[0] = tile(first, first // 2, True)
        acc[1] = tile(second, second // 2, True)
        for n in range(7):
            in_first = n < near
            slot = jnp.where(in_first, 0, 1)
            block = jnp.where(in_first, first, second)
            chunk = jnp.where(in_first, n, n - near)
            acc[slot] += tile(block, chunk, False)
        for s, block in enumerate((first, second)):
            both = acc[s]
            result = (both[:, 0:HD] / both[:, HD : 2 * HD]).astype(BF16)
            result = jnp.concatenate([result[0:BLK], result[BLK : 2 * BLK]], axis=1)

            @pl.when(block == head)
            def _():
                gathered[0, t, half] = result

            @pl.when(block != head)
            def _():
                stage[t, s] = result
                a_copy(t, s, block).start()

    def source(u, s):
        return lax.rem(pair - u + 8, 8) + 8 * s

    core_copy(0).start()

    def step(t, _):
        @pl.when(t < STEPS)
        def _():
            w_copy(0, t).start()
            w_copy(1, t).start()
            attend(t)

        @pl.when(jnp.logical_and(t >= 1, t < STEPS + 1))
        def _():
            u = t - 1
            for s in range(2):
                @pl.when(source(u, s) != head)
                def _():
                    a_arrival(u, s).wait_recv()
            x_copy(0, u).start()
            x_copy(1, u).start()

        @pl.when(t >= 2)
        def _():
            u = t - 2
            for way in range(2):
                x_copy(way, u).wait_recv()
                f_copy(way, u).start()

        return 0

    lax.fori_loop(0, STEPS + 2, step, 0)

    loads[3].wait()
    group = lane_group(128)

    def pack(n, _):
        rows = pl.multiple_of(n * 128, 128)
        parts = []
        for g in range(4):
            part = w_ref[pl.ds(g * 1024 + rows, 128), MAIN:FEAT].astype(F32)
            part = jnp.concatenate([part, jnp.zeros((128, 128 - REM), F32)], axis=1)
            parts.append(roll(part, REM * g))
        pk[0, pl.ds(rows, 128), :] = merge_lanes(parts, group).astype(BF16)
        return 0

    lax.fori_loop(0, 8, pack, 0)
    core_copy(1).start()
    p_copy(0).start()
    p_copy(1).start()

    def w_arrive(n, _):
        w_copy(0, n).wait_recv()
        w_copy(1, n).wait_recv()
        return 0

    lax.fori_loop(0, STEPS, w_arrive, 0)
    core_copy(2).start()
    p_copy(0).wait_recv()
    p_copy(1).wait_recv()
    core_copy(3).start()
    for n in (0, 1, 3, 2):
        core_copy(n).wait_recv()

    def spread(n, _):
        rows = pl.multiple_of(n * 128, 128)
        parts = [pk[g, pl.ds(rows, 128), :].astype(F32) for g in range(4)]
        for a in range(4):
            merged = merge_lanes([roll(parts[g], REM * (g - a)) for g in range(4)], group)
            rem_w[pl.ds(a * 1024 + rows, 128), :] = merged.astype(BF16)
        return 0

    lax.fori_loop(0, 8, spread, 0)

    def project(total, lhs_of):
        total[...] = jnp.zeros_like(total)

        def add(u, _):
            parts = [None] * 5
            for s in range(2):
                rows = pl.ds(pl.multiple_of(source(u, s) * 256, 256), 256)
                lhs = lhs_of(u, s)
                for n in range(5):
                    if n == 0:
                        rhs = w_ref[rows, 0:MAIN]
                    elif n == 4:
                        rhs = rem_w[rows, :]
                    else:
                        rhs = wm[n - 1, rows, :]
                    term = jnp.dot(lhs, rhs, preferred_element_type=F32)
                    parts[n] = term if parts[n] is None else parts[n] + term
            for n in range(5):
                cols = pl.ds(n * 256, 256 if n < 4 else 128)
                total[:, cols] += parts[n]
            return 0

        lax.fori_loop(0, STEPS, add, 0)

    small = lane_group(16)
    places = (x, lax.rem(x + 3, 4), lax.rem(x + 1, 4), lax.rem(x + 2, 4))

    def o_copy(n, slot):
        row = places[slot] * 4 + low
        return copy_to(
            ostage.at[n - 1, slot], obuf.at[row], o_send.at[n - 1, slot], o_recv.at[n - 1, slot], mates[n], head
        )

    def o_arrival(n, slot):
        row = places[slot] * 4 + lax.rem(mates[n], 4)
        return copy_to(
            ostage.at[n - 1, slot], obuf.at[row], o_send.at[n - 1, slot], o_recv.at[n - 1, slot], mates[n], head
        )

    def emit(total, base, slot):
        at = base * BLK
        rest = total[at : at + BLK, 1024:1152]
        for n in (2, 3, 1):
            ostage[n - 1, slot, 0:BLK, :] = total[at : at + BLK, n * 256 : (n + 1) * 256].astype(BF16)
            for side in range(2):
                parts = [
                    roll(rest[16 * (4 * side + g) : 16 * (4 * side + g) + 16], REM * (g - n)) for g in range(4)
                ]
                ostage[n - 1, slot, BLK:OROWS, side * 128 : side * 128 + 128] = merge_lanes(parts, small).astype(BF16)
            o_copy(n, slot).start()
        row = places[slot] * 4 + low
        out_ref[row, :, 0:MAIN] = total[at : at + BLK, 0:256].astype(BF16)
        out_ref[row, :, MAIN:FEAT] = rest[:, 0:REM].astype(BF16)

    project(acc1, lambda u, s: gathered[0:3, u, s].reshape(3 * BLK, 256))
    for slot in range(3):
        emit(acc1, slot, slot)

    def f_arrive(u, _):
        f_copy(0, u).wait_recv()
        f_copy(1, u).wait_recv()
        return 0

    lax.fori_loop(0, STEPS, f_arrive, 0)
    project(acc2, lambda u, s: gathered[3, u, s])
    emit(acc2, 0, 3)

    for slot in range(4):
        for n in range(1, 4):
            o_arrival(n, slot).wait_recv()
            row = places[slot] * 4 + lax.rem(mates[n], 4)
            out_ref[row, :, 0:MAIN] = obuf[row, 0:BLK, :]
            for side in range(2):
                packed = obuf[row, BLK:OROWS, side * 128 : side * 128 + 128].astype(F32)
                for g in range(4):
                    at = 16 * (4 * side + g)
                    out_ref[row, at : at + 16, MAIN:FEAT] = roll(packed, -REM * g)[:, 0:REM].astype(BF16)

    def sent(t, _):
        j = lax.rem(head + t, 8)
        first = jnp.where(half == 0, j, 15 - j)
        for s, block in enumerate((first, 15 - first)):
            @pl.when(block != head)
            def _():
                a_copy(t, s, block).wait_send()
        for way in range(2):
            x_copy(way, t).wait_send()
            f_copy(way, t).wait_send()
            w_copy(way, t).wait_send()
        return 0

    lax.fori_loop(0, STEPS, sent, 0)
    for n in range(4):
        core_copy(n).wait_send()
    p_copy(0).wait_send()
    p_copy(1).wait_send()
    for slot in range(4):
        for n in range(1, 4):
            o_copy(n, slot).wait_send()


def body(queries, keys, values, doc_lengths, out_weight):
    dma = pltpu.SemaphoreType.DMA
    anywhere = pl.BlockSpec(memory_space=pl.ANY)
    return pl.pallas_call(
        kernel,
        out_shape=jax.ShapeDtypeStruct((16, BLK, FEAT), BF16),
        in_specs=[anywhere, anywhere, anywhere, pl.BlockSpec(memory_space=pltpu.SMEM), anywhere],
        out_specs=pl.BlockSpec(memory_space=pltpu.VMEM),
        scratch_shapes=[
            pltpu.VMEM((SEQ, 2 * HD), BF16),
            pltpu.VMEM((SEQ, HD), BF16),
            pltpu.VMEM((SEQ, HD), BF16),
            pltpu.VMEM((DEPTH, FEAT), BF16),
            pltpu.SMEM((16,), jnp.int32),
            pltpu.VMEM((2, 2 * BLK, 2 * HD), F32),
            pltpu.VMEM((STEPS, 2, BLK, 256), BF16),
            pltpu.VMEM((4, STEPS, 2, BLK, 256), BF16),
            pltpu.VMEM((3, DEPTH, MAIN), BF16),
            pltpu.VMEM((4, 1024, 128), BF16),
            pltpu.VMEM((DEPTH, 128), BF16),
            pltpu.VMEM((3 * BLK, 1152), F32),
            pltpu.VMEM((BLK, 1152), F32),
            pltpu.VMEM((3, 4, OROWS, 256), BF16),
            pltpu.VMEM((16, OROWS, 256), BF16),
            dma((4,)),
            dma((STEPS, 2)), dma((STEPS, 2)),
            dma((2, STEPS)), dma((2, STEPS)),
            dma((2, STEPS)), dma((2, STEPS)),
            dma((2, STEPS)), dma((2, STEPS)),
            dma((2,)), dma((2,)),
            dma((4,)), dma((4,)),
            dma((3, 4)), dma((3, 4)),
        ],
        compiler_params=pltpu.CompilerParams(
            collective_id=0, has_side_effects=True, vmem_limit_bytes=56 * 1024 * 1024
        ),
    )(queries, keys, values, doc_lengths, out_weight)


def solution(mesh):
    return jax.shard_map(
        body,
        mesh=mesh,
        in_specs=(P("dp", "head"), P("dp", "head"), P("dp", "head"), P(), P(None, "dp")),
        out_specs=P(None, "head", "dp"),
        check_vma=False,
    )
```

time: 234 us -> 96.2 us (0.41)
  waiting for transfers between devices: 120 us -> 0 us
  Pallas kernels: 0 us -> 88.9 us
  blocking collectives: 33 us -> 0 us
  matrix products: 28.6 us -> 0 us
  between operations: 21.6 us -> 0.01 us
  local copies, waits for them, and re-layouts: 21.6 us -> 7 us
  other arithmetic: 9.03 us -> 0 us
    all_gather x1 -> x0, waiting for transfers between devices: 120 us -> none  [body(): lax.all_gather(regrouped, 'dp', axis=0, tiled=True)]
    pallas_call x0 -> x1, Pallas kernels: none -> 88.9 us  [body(): pl.pallas_call(kernel, out_shape=jax.ShapeDtypeStruct((16, BLK, FEAT), BF...]
    all_to_all x1 -> x0, blocking collectives: 33 us -> none  [body(): lax.all_to_all(attended.reshape(head_count, part_rows, features), 'head',...]
    dot_general x13 -> x0, matrix products: 28.6 us -> none  [the longest x6 12.4 us: add_tile(): jnp.einsum('qhgd,phd->hgqp', query_block, key_block, preferred_element_ty...]
    slice x5 -> x0, local copies, waits for them, and re-layouts: 6.09 us -> none  [the longest x1 1.96 us: body(): query_heads[row_block * BLK:(row_block + 1) * BLK]]
    and x4 -> x0, other arithmetic: 5.23 us -> none  [add_tile(): (q_doc[:, None] == k_doc[None, :]) & (q_pos[:, None] >= k_pos[None, :])]
    reshape x5 -> x0, local copies, waits for them, and re-layouts: 4.84 us -> none  [the longest x4 3.63 us: attend_block(): return result.reshape(BLK, kv_heads * group_size * HD)]
    pallas_call x0 -> x1, local copies, waits for them, and re-layouts: none -> 2.51 us  [body(): pl.pallas_call(kernel, out_shape=jax.ShapeDtypeStruct((16, BLK, FEAT), BF...]
  transfers between devices with their start and end apart: 1 -> 0, of which waited for: 1 -> 0; matrix products, arithmetic and copies ran while one was open for 0% -> 0% of each run, Pallas kernels for 0% -> 0%
where the time goes in v1:
time: 96.2 us; the launch traced here: 96 us
  Pallas kernels  88.9 us (92%)
  local copies, waits for them, and re-layouts  7 us (7%)
    pallas_call x1, Pallas kernels, body(): pl.pallas_call(kernel, out_shape=jax.ShapeDtypeStruct((16, BLK, FEAT), BF...  88.9 us
    unnamed x1, local copies, waits for them, and re-layouts  4.49 us
    pallas_call x1, local copies, waits for them, and re-layouts, body(): pl.pallas_call(kernel, out_shape=jax.ShapeDtypeStruct((16, BLK, FEAT), BF...  2.51 us

profile of v1, /device:TPU:1, one launch (start us, length us, event | category | flops | bytes accessed | tf_op | source)
XLA Modules:
  0.0 96.0 jit_solution(10555784213279185396)
XLA Ops:
  0.0 4.5 %copy.6.w_hbm = bf16[4096,288]{1,0:T(8,128)(2,1)} copy(bf16[4096,288]{0,1:T(8,128)(2,1)} %param.9) | data formatting | bytes 4718592 | tf_op args[4]
  4.5 88.9 %shard_map.55 = bf16[16,128,288]{2,1,0:T(8,128)(2,1)} custom-call(bf16[2048,256]{1,0:T(8,128)(2,1)} %q_hbm.1, bf16[2048,128]{1,0:T(8,128)(2,1)} %k_hbm.1, bf16[2048,128]{1,0:T(8,128)(2,1)} %v_hbm.1, s32[16,16]{1,0:T(8,128)} %doc_ref.1, bf16[4096,288]{1,0:T(8,128)(2,1)} %copy.6.w_hbm), custom_call_target="tpu_custom_call" | custom-call | tf_op jit(solution)/shard_map/pallas_call | solution.py:381
  93.5 2.5 %copy.7 = bf16[16,128,288]{1,2,0:T(8,128)(2,1)} copy(bf16[16,128,288]{2,1,0:T(8,128)(2,1)} %shard_map.55) | data formatting | bytes 2359296 | tf_op jit(solution)/shard_map/pallas_call | solution.py:381

commit v2 on v0

v2 whole, which is shorter than its diff:
```python
import math

import jax
import jax.numpy as jnp
from jax import lax
from jax.experimental import pallas as pl
from jax.experimental.pallas import tpu as pltpu
from jax.sharding import PartitionSpec as P

HD = 128
BLK = 128
SEQ = 2048
CHUNK = 256
FEAT = 288
HEADS = 16
EARLY = 2
LAG_A, LAG_W, LAG_Z, LAG_X = 6, 16, 20, 10
SCALE = 1.0 / 12.0 / 50.0
GAIN = 50.0 * math.log2(math.e)
MESH = pl.DeviceIdType.MESH
F32 = jnp.float32
BF16 = jnp.bfloat16


def kernel(
    q_hbm, k_hbm, v_hbm, doc_ref, w_hbm, out_ref,
    q_ref, k_ref, v_ref, block_doc,
    acc, stage, gathered, wt, total, ostage,
    ld_sem, l_sem, a_send, a_recv, x_send, x_recv, f_send, f_recv,
    w_send, w_recv, z_send, z_recv, s_send, s_recv, m_send, m_recv, o_send, o_recv,
):
    dp, head = lax.axis_index("dp"), lax.axis_index("head")
    x, low = dp // 4, lax.rem(dp, 4)
    z, y_high = head // 2, lax.rem(head, 2)
    odd = lax.rem(z, 2)
    right = lax.rem(x + 1, 4) * 4 + low
    left = lax.rem(x + 3, 4) * 4 + low
    core_mate = dp + 1 - 2 * lax.rem(dp, 2)
    y_mate = dp + 2 - 4 * lax.rem(dp // 2, 2)
    both_mate = core_mate + 2 - 4 * lax.rem(dp // 2, 2)
    head_mate = head + 1 - 2 * y_high
    mates = (dp, core_mate, y_mate, both_mate)

    def copy_to(src, dst, send, recv, to_dp, to_head):
        return pltpu.make_async_remote_copy(
            src_ref=src, dst_ref=dst, send_sem=send, recv_sem=recv,
            device_id={"dp": to_dp, "head": to_head}, device_id_type=MESH,
        )

    def shifted(k, sign):
        far = (k + 2) // 4
        up = jnp.where(lax.rem(k, 2) == 0, far, 8 - far)
        across = jnp.where((far == 0) | (far == 4), lax.rem(k, 2), lax.rem(k // 2 + 1, 2))
        return lax.rem(z + 8 + sign * up, 8) * 2 + lax.rem(y_high + across, 2)

    loads = [
        pltpu.make_async_copy(q_hbm, q_ref, ld_sem.at[0]),
        pltpu.make_async_copy(k_hbm, k_ref, ld_sem.at[1]),
        pltpu.make_async_copy(v_hbm, v_ref, ld_sem.at[2]),
    ]
    for load in loads:
        load.start()

    def w_load(n):
        cols = pl.ds(pl.multiple_of(n * 256, 256), 256)
        return pltpu.make_async_copy(w_hbm.at[:, cols], wt.at[n, pl.ds(0, FEAT)], l_sem.at[n])

    def start_load(n, _):
        w_load(n).start()
        return 0

    lax.fori_loop(0, HEADS, start_load, 0)
    barrier = pltpu.get_barrier_semaphore()

    def greet(to_dp, to_head):
        pl.semaphore_signal(barrier, inc=1, device_id={"dp": to_dp, "head": to_head}, device_id_type=MESH)

    def greet_heads(n, _):
        greet(dp, lax.rem(head + n, HEADS))
        return 0

    lax.fori_loop(1, HEADS, greet_heads, 0)
    greet(right, head)
    greet(left, head)
    greet(core_mate, head)
    greet(y_mate, head)
    greet(both_mate, head)
    greet(y_mate, head_mate)

    ends = []
    end = jnp.int32(0)
    for n in range(16):
        end = end + doc_ref[dp, n]
        ends.append(end)

    def number(b, _):
        count = jnp.int32(0)
        for end in ends:
            count = count + jnp.where(end <= b * BLK, 1, 0).astype(jnp.int32)
        block_doc[b] = count
        return 0

    lax.fori_loop(0, 16, number, 0)
    for load in loads:
        load.wait()

    differences = lax.rem(lax.broadcasted_iota(jnp.int32, (2 * BLK, CHUNK), 0), BLK) - lax.broadcasted_iota(
        jnp.int32, (2 * BLK, CHUNK), 1
    )

    def tile(q_two, block, chunk, diagonal):
        cols = pl.ds(pl.multiple_of(chunk * CHUNK, CHUNK), CHUNK)
        raw = lax.dot_general(q_two, k_ref[cols, :], (((1,), (1,)), ((), ())), preferred_element_type=F32)
        weight = jnp.exp2(jnp.tanh(raw * SCALE) * GAIN)
        if diagonal:
            weight = jnp.where(differences >= chunk * CHUNK - block * BLK, weight, 0.0)
        own = block_doc[block]
        live = []
        for n in range(2):
            on = block_doc[2 * chunk + n] == own
            if not diagonal:
                on = jnp.logical_and(on, chunk < block // 2)
            live.append(jnp.full((BLK, HD), jnp.where(on, 1.0, 0.0).astype(F32), F32).astype(BF16))
        live = jnp.concatenate(live, axis=0)
        value_two = jnp.concatenate([v_ref[cols, :] * live, live], axis=1)
        return jnp.dot(weight.astype(BF16), value_two, preferred_element_type=F32)

    def attend(k, block, into):
        rows = pl.ds(pl.multiple_of(block * BLK, BLK), BLK)

        def tiles(others):
            q_two = jnp.concatenate([q_ref[rows, 0:HD], q_ref[rows, HD : 2 * HD]], axis=0)
            both = tile(q_two, block, block // 2, True)
            for n in range(others):
                both = both + tile(q_two, block, n, False)
            acc[...] = both

        pl.when(block < 8)(lambda: tiles(3))
        pl.when(block >= 8)(lambda: tiles(7))
        both = acc[...]
        result = (both[:, 0:HD] / both[:, HD : 2 * HD]).astype(BF16)
        into[...] = jnp.concatenate([result[0:BLK], result[BLK : 2 * BLK]], axis=1)

    def a_copy(k):
        return copy_to(stage.at[k], gathered.at[0, k], a_send.at[k], a_recv.at[k], dp, shifted(k, 1))

    def x_copy(way, k):
        return copy_to(
            gathered.at[0, k], gathered.at[1 + way, k], x_send.at[way, k], x_recv.at[way, k],
            right if way == 0 else left, head,
        )

    def f_copy(k):
        way = lax.rem(k, 2)
        return copy_to(
            gathered.at[1 + way, k], gathered.at[3, k], f_send.at[k], f_recv.at[k],
            jnp.where(way == 0, right, left), head,
        )

    own_rows, mate_rows, far_rows, both_rows = (pl.ds(n * FEAT, FEAT) for n in range(4))

    def w_copy(n):
        c = 2 * n + odd
        return copy_to(
            wt.at[c, own_rows], wt.at[c, far_rows], w_send.at[n], w_recv.at[n],
            y_mate, jnp.where(lax.rem(n, 2) == 0, head, head_mate),
        )

    def z_copy(n, parity):
        c = 2 * n + parity
        up = jnp.where(lax.rem(n // 2, 2) == 0, 1, 7)
        return copy_to(
            wt.at[c, far_rows], wt.at[c, far_rows], z_send.at[n], z_recv.at[n], dp, lax.rem(z + up, 8) * 2 + y_high
        )

    def s_copy(c):
        return copy_to(wt.at[c, far_rows], wt.at[c, both_rows], s_send.at[c], s_recv.at[c], core_mate, head)

    m_copy = copy_to(wt.at[:, own_rows], wt.at[:, mate_rows], m_send, m_recv, core_mate, head)

    attend(0, head, gathered.at[0, 0])

    def early(k, _):
        attend(k, shifted(k, 1), stage.at[k])
        return 0

    lax.fori_loop(1, EARLY, early, 0)

    def end_load(n, _):
        w_load(n).wait()
        return 0

    lax.fori_loop(0, HEADS, end_load, 0)
    pl.semaphore_wait(barrier, 21)

    def early_send(k, _):
        a_copy(k).start()
        return 0

    lax.fori_loop(1, EARLY, early_send, 0)

    def send_w(n, _):
        w_copy(n).start()
        return 0

    lax.fori_loop(0, 8, send_w, 0)
    m_copy.start()

    def step(t, _):
        @pl.when(t < HEADS)
        def _():
            attend(t, shifted(t, 1), stage.at[t])
            a_copy(t).start()

        def during(lag, count, act):
            k = t - lag
            pl.when(jnp.logical_and(k >= 0, k < count))(lambda: act(k))

        def pass_own(k):
            @pl.when(k > 0)
            def _():
                a_copy(k).wait_recv()
            x_copy(0, k).start()
            x_copy(1, k).start()

        def pass_w(n):
            w_copy(n).wait_recv()
            z_copy(n, odd).start()
            s_copy(2 * n + odd).start()

        def pass_z(n):
            z_copy(n, 1 - odd).wait_recv()
            s_copy(2 * n + 1 - odd).start()

        def pass_far(k):
            x_copy(0, k).wait_recv()
            x_copy(1, k).wait_recv()
            f_copy(k).start()

        during(LAG_A, HEADS, pass_own)
        during(LAG_W, 8, pass_w)
        during(LAG_Z, 8, pass_z)
        during(LAG_X, HEADS, pass_far)
        return 0

    lax.fori_loop(EARLY, max(HEADS + LAG_X, 8 + LAG_Z), step, 0)

    def w_arrive(c, _):
        s_copy(c).wait_recv()
        return 0

    lax.fori_loop(0, HEADS, w_arrive, 0)
    m_copy.wait_recv()

    def project(slots, width):
        into = total.at[:, pl.ds(0, width)]
        into[...] = jnp.zeros((4 * FEAT, width), F32)

        def add(u, _):
            term = None
            for s in range(2):
                k = 2 * u + s
                if slots == (3,):
                    f_copy(k).wait_recv()
            for s in range(2):
                k = 2 * u + s
                rhs = jnp.concatenate([gathered[n, k] for n in slots], axis=0)
                part = lax.dot_general(
                    wt[shifted(k, -1)], rhs, (((1,), (1,)), ((), ())), preferred_element_type=F32
                )
                term = part if term is None else term + part
            into[...] += term
            return 0

        lax.fori_loop(0, 8, add, 0)

    places = (x, lax.rem(x + 3, 4), lax.rem(x + 1, 4), lax.rem(x + 2, 4))

    def o_copy(n, slot):
        row = places[slot] * 4 + low
        return copy_to(
            ostage.at[n, slot], out_ref.at[row], o_send.at[n, slot], o_recv.at[n, slot], mates[n], head
        )

    def o_own(slot):
        return pltpu.make_async_copy(ostage.at[0, slot], out_ref.at[places[slot] * 4 + low], o_send.at[0, slot])

    def o_arrival(n, slot):
        row = places[slot] * 4 + lax.rem(mates[n], 4)
        return copy_to(
            ostage.at[n, slot], out_ref.at[row], o_send.at[n, slot], o_recv.at[n, slot], mates[n], head
        )

    def emit(slots):
        for n in (2, 3, 1, 0):
            for at, slot in enumerate(slots):
                ostage[n, slot] = total[n * FEAT : (n + 1) * FEAT, at * BLK : (at + 1) * BLK].astype(BF16)
                if n:
                    o_copy(n, slot).start()
                else:
                    o_own(slot).start()

    for slots in ((0,), (1, 2), (3,)):
        project(slots, len(slots) * BLK)
        emit(slots)

    for slot in range(4):
        for n in range(1, 4):
            o_arrival(n, slot).wait_recv()
            o_copy(n, slot).wait_send()
        o_own(slot).wait()

    def sent(k, _):
        @pl.when(k > 0)
        def _():
            a_copy(k).wait_send()
        x_copy(0, k).wait_send()
        x_copy(1, k).wait_send()
        f_copy(k).wait_send()
        s_copy(k).wait_send()
        @pl.when(k < 8)
        def _():
            w_copy(k).wait_send()
            z_copy(k, odd).wait_send()
        return 0

    lax.fori_loop(0, HEADS, sent, 0)
    m_copy.wait_send()


def body(queries, keys, values, doc_lengths, out_weight):
    dma = pltpu.SemaphoreType.DMA
    anywhere = pl.BlockSpec(memory_space=pl.ANY)
    mixed = pl.pallas_call(
        kernel,
        out_shape=jax.ShapeDtypeStruct((16, FEAT, BLK), BF16),
        in_specs=[anywhere, anywhere, anywhere, pl.BlockSpec(memory_space=pltpu.SMEM), anywhere],
        out_specs=anywhere,
        scratch_shapes=[
            pltpu.VMEM((SEQ, 2 * HD), BF16),
            pltpu.VMEM((SEQ, HD), BF16),
            pltpu.VMEM((SEQ, HD), BF16),
            pltpu.SMEM((16,), jnp.int32),
            pltpu.VMEM((2 * BLK, 2 * HD), F32),
            pltpu.VMEM((HEADS, BLK, 256), BF16),
            pltpu.VMEM((4, HEADS, BLK, 256), BF16),
            pltpu.VMEM((HEADS, 4 * FEAT, 256), BF16),
            pltpu.VMEM((4 * FEAT, 2 * BLK), F32),
            pltpu.VMEM((4, 4, FEAT, BLK), BF16),
            dma((3,)), dma((HEADS,)),
            dma((HEADS,)), dma((HEADS,)),
            dma((2, HEADS)), dma((2, HEADS)),
            dma((HEADS,)), dma((HEADS,)),
            dma((8,)), dma((8,)),
            dma((8,)), dma((8,)),
            dma((HEADS,)), dma((HEADS,)),
            dma, dma,
            dma((4, 4)), dma((4, 4)),
        ],
        compiler_params=pltpu.CompilerParams(
            collective_id=0, has_side_effects=True, vmem_limit_bytes=56 * 1024 * 1024
        ),
    )(queries, keys, values, doc_lengths, out_weight.T)
    return mixed.transpose(0, 2, 1)


def solution(mesh):
    return jax.shard_map(
        body,
        mesh=mesh,
        in_specs=(P("dp", "head"), P("dp", "head"), P("dp", "head"), P(), P(None, "dp")),
        out_specs=P(None, "head", "dp"),
        check_vma=False,
    )
```

time: 234 us -> 75.7 us (0.32)
  waiting for transfers between devices: 120 us -> 0 us
  Pallas kernels: 0 us -> 73.1 us
  blocking collectives: 33 us -> 0 us
  matrix products: 28.6 us -> 0 us
  between operations: 21.6 us -> 0.01 us
  local copies, waits for them, and re-layouts: 21.6 us -> 2.36 us
  other arithmetic: 9.03 us -> 0 us
    all_gather x1 -> x0, waiting for transfers between devices: 120 us -> none  [body(): lax.all_gather(regrouped, 'dp', axis=0, tiled=True)]
    pallas_call x0 -> x1, Pallas kernels: none -> 73.1 us  [body(): pl.pallas_call(kernel, out_shape=jax.ShapeDtypeStruct((16, FEAT, BLK), BF...]
    all_to_all x1 -> x0, blocking collectives: 33 us -> none  [body(): lax.all_to_all(attended.reshape(head_count, part_rows, features), 'head',...]
    dot_general x13 -> x0, matrix products: 28.6 us -> none  [the longest x6 12.4 us: add_tile(): jnp.einsum('qhgd,phd->hgqp', query_block, key_block, preferred_element_ty...]
    slice x5 -> x0, local copies, waits for them, and re-layouts: 6.09 us -> none  [the longest x1 1.96 us: body(): query_heads[row_block * BLK:(row_block + 1) * BLK]]
    and x4 -> x0, other arithmetic: 5.23 us -> none  [add_tile(): (q_doc[:, None] == k_doc[None, :]) & (q_pos[:, None] >= k_pos[None, :])]
    reshape x5 -> x0, local copies, waits for them, and re-layouts: 4.84 us -> none  [the longest x4 3.63 us: attend_block(): return result.reshape(BLK, kv_heads * group_size * HD)]
    unnamed x33 -> x1, local copies, waits for them, and re-layouts: 4.95 us -> 2.36 us
  transfers between devices with their start and end apart: 1 -> 0, of which waited for: 1 -> 0; matrix products, arithmetic and copies ran while one was open for 0% -> 0% of each run, Pallas kernels for 0% -> 0%
where the time goes in v2:
time: 75.7 us; the launch traced here: 75.5 us
  Pallas kernels  73.1 us (97%)
  local copies, waits for them, and re-layouts  2.36 us (3%)
    pallas_call x1, Pallas kernels, body(): pl.pallas_call(kernel, out_shape=jax.ShapeDtypeStruct((16, FEAT, BLK), BF...  73.1 us
    unnamed x1, local copies, waits for them, and re-layouts  2.36 us

profile of v2, /device:TPU:1, one launch (start us, length us, event | category | flops | bytes accessed | tf_op | source)
XLA Modules:
  0.0 75.5 jit_solution(15795002736363572758)
XLA Ops:
  0.0 73.1 %shard_map.55 = bf16[16,288,128]{2,1,0:T(8,128)(2,1)} custom-call(bf16[2048,256]{1,0:T(8,128)(2,1)} %q_hbm.1, bf16[2048,128]{1,0:T(8,128)(2,1)} %k_hbm.1, bf16[2048,128]{1,0:T(8,128)(2,1)} %v_hbm.1, s32[16,16]{1,0:T(8,128)} %doc_ref.1, bf16[288,4096]{1,0:T(8,128)(2,1)} %bitcast.3), custom_call_target="tpu_custom_call" | custom-call | tf_op jit(solution)/shard_map/pallas_call | solution.py:334
  73.2 2.4 %copy.7 = bf16[16,128,288]{1,2,0:T(8,128)(2,1)} copy(bf16[16,128,288]{1,2,0:T(8,128)(2,1)} %bitcast.2) | data formatting | bytes 2359296

commit v3 on v2

--- a/solution.py
+++ b/solution.py
@@ -13,8 +13,13 @@
 CHUNK = 256
 FEAT = 288
 HEADS = 16
+READY = 6
 EARLY = 2
-LAG_A, LAG_W, LAG_Z, LAG_X = 6, 16, 20, 10
+PART = FEAT // 2
+RELAY = 4
+CHUNKS = 8
+FAR_A, BOTH_A, OWN, MATE, FAR_B, BOTH_B = 0, PART, FEAT, 2 * FEAT, 3 * FEAT, 3 * FEAT + PART
+LAG_A, LAG_W, LAG_Z, LAG_X = 5, 15, 20, 14
 SCALE = 1.0 / 12.0 / 50.0
 GAIN = 50.0 * math.log2(math.e)
 MESH = pl.DeviceIdType.MESH
@@ -63,7 +68,7 @@
 
     def w_load(n):
         cols = pl.ds(pl.multiple_of(n * 256, 256), 256)
-        return pltpu.make_async_copy(w_hbm.at[:, cols], wt.at[n, pl.ds(0, FEAT)], l_sem.at[n])
+        return pltpu.make_async_copy(w_hbm.at[:, cols], wt.at[n, pl.ds(OWN, FEAT)], l_sem.at[n])
 
     def start_load(n, _):
         w_load(n).start()
@@ -157,12 +162,16 @@
             jnp.where(way == 0, right, left), head,
         )
 
-    own_rows, mate_rows, far_rows, both_rows = (pl.ds(n * FEAT, FEAT) for n in range(4))
-
-    def w_copy(n):
-        c = 2 * n + odd
-        return copy_to(
-            wt.at[c, own_rows], wt.at[c, far_rows], w_send.at[n], w_recv.at[n],
+    def piece(c, row, count):
+        return wt.at[pl.ds(2 * c, 2), pl.ds(row, count)]
+
+    def w_chunk(n):
+        return jnp.where(n < RELAY, 2 * n + odd, n - RELAY)
+
+    def w_copy(n, part):
+        c = w_chunk(n)
+        return copy_to(
+            piece(c, OWN + part * PART, PART), piece(c, FAR_B if part else FAR_A, PART), w_send.at[n], w_recv.at[n],
             y_mate, jnp.where(lax.rem(n, 2) == 0, head, head_mate),
         )
 
@@ -170,13 +179,19 @@
         c = 2 * n + parity
         up = jnp.where(lax.rem(n // 2, 2) == 0, 1, 7)
         return copy_to(
-            wt.at[c, far_rows], wt.at[c, far_rows], z_send.at[n], z_recv.at[n], dp, lax.rem(z + up, 8) * 2 + y_high
-        )
-
-    def s_copy(c):
-        return copy_to(wt.at[c, far_rows], wt.at[c, both_rows], s_send.at[c], s_recv.at[c], core_mate, head)
-
-    m_copy = copy_to(wt.at[:, own_rows], wt.at[:, mate_rows], m_send, m_recv, core_mate, head)
+            piece(c, FAR_A, PART), piece(c, FAR_A, PART), z_send.at[n], z_recv.at[n],
+            dp, lax.rem(z + up, 8) * 2 + y_high,
+        )
+
+    def s_copy(c, part):
+        return copy_to(
+            piece(c, FAR_B if part else FAR_A, PART), piece(c, BOTH_B if part else BOTH_A, PART),
+            s_send.at[part, c], s_recv.at[part, c], core_mate, head,
+        )
+
+    m_copy = copy_to(
+        wt.at[:, pl.ds(OWN, FEAT)], wt.at[:, pl.ds(MATE, FEAT)], m_send, m_recv, core_mate, head
+    )
 
     attend(0, head, gathered.at[0, 0])
 
@@ -191,6 +206,7 @@
         return 0
 
     lax.fori_loop(0, HEADS, end_load, 0)
+    total[OWN : OWN + 2 * FEAT, 0 : 3 * BLK] = jnp.zeros((2 * FEAT, 3 * BLK), F32)
     pl.semaphore_wait(barrier, 21)
 
     def early_send(k, _):
@@ -200,10 +216,10 @@
     lax.fori_loop(1, EARLY, early_send, 0)
 
     def send_w(n, _):
-        w_copy(n).start()
-        return 0
-
-    lax.fori_loop(0, 8, send_w, 0)
+        w_copy(n, 0).start()
+        return 0
+
+    lax.fori_loop(0, RELAY, send_w, 0)
     m_copy.start()
 
     def step(t, _):
@@ -224,90 +240,120 @@
             x_copy(1, k).start()
 
         def pass_w(n):
-            w_copy(n).wait_recv()
+            w_copy(n, 0).wait_recv()
+            w_copy(RELAY + 2 * n, 1).start()
+            w_copy(RELAY + 2 * n + 1, 1).start()
             z_copy(n, odd).start()
-            s_copy(2 * n + odd).start()
+            s_copy(2 * n + odd, 0).start()
 
         def pass_z(n):
             z_copy(n, 1 - odd).wait_recv()
-            s_copy(2 * n + 1 - odd).start()
+            s_copy(2 * n + 1 - odd, 0).start()
 
         def pass_far(k):
             x_copy(0, k).wait_recv()
             x_copy(1, k).wait_recv()
             f_copy(k).start()
+            pl.when(k == 0)(lambda: m_copy.wait_recv())
+            rhs = jnp.concatenate([gathered[n, k] for n in range(3)], axis=0)
+            total[OWN : OWN + 2 * FEAT, 0 : 3 * BLK] += lax.dot_general(
+                wt[shifted(k, -1), OWN : OWN + 2 * FEAT, :], rhs, (((1,), (1,)), ((), ())),
+                preferred_element_type=F32,
+            )
 
         during(LAG_A, HEADS, pass_own)
-        during(LAG_W, 8, pass_w)
-        during(LAG_Z, 8, pass_z)
+        during(LAG_W, RELAY, pass_w)
+        during(LAG_Z, RELAY, pass_z)
         during(LAG_X, HEADS, pass_far)
         return 0
 
-    lax.fori_loop(EARLY, max(HEADS + LAG_X, 8 + LAG_Z), step, 0)
-
-    def w_arrive(c, _):
-        s_copy(c).wait_recv()
-        return 0
-
-    lax.fori_loop(0, HEADS, w_arrive, 0)
-    m_copy.wait_recv()
-
-    def project(slots, width):
-        into = total.at[:, pl.ds(0, width)]
-        into[...] = jnp.zeros((4 * FEAT, width), F32)
+    lax.fori_loop(EARLY, max(HEADS + LAG_X, RELAY + LAG_Z), step, 0)
+
+    def w_direct(n, _):
+        w_copy(n, 1).wait_recv()
+        s_copy(w_chunk(n), 1).start()
+        return 0
+
+    def w_arrive(part):
+        def one(c, _):
+            s_copy(c, part).wait_recv()
+            return 0
+
+        lax.fori_loop(0, CHUNKS, one, 0)
+
+    def project(slots, first, count, start=0, stop=8, arriving=False):
+        into = total.at[pl.ds(first, count), pl.ds(slots[0] * BLK, len(slots) * BLK)]
+        if start == 0:
+            into[...] = jnp.zeros((count, len(slots) * BLK), F32)
 
         def add(u, _):
+            if arriving:
+                f_copy(2 * u).wait_recv()
+                f_copy(2 * u + 1).wait_recv()
             term = None
-            for s in range(2):
-                k = 2 * u + s
-                if slots == (3,):
-                    f_copy(k).wait_recv()
             for s in range(2):
                 k = 2 * u + s
                 rhs = jnp.concatenate([gathered[n, k] for n in slots], axis=0)
                 part = lax.dot_general(
-                    wt[shifted(k, -1)], rhs, (((1,), (1,)), ((), ())), preferred_element_type=F32
+                    wt[shifted(k, -1), first : first + count, :], rhs, (((1,), (1,)), ((), ())),
+                    preferred_element_type=F32,
                 )
                 term = part if term is None else term + part
             into[...] += term
             return 0
 
-        lax.fori_loop(0, 8, add, 0)
+        lax.fori_loop(start, stop, add, 0)
 
     places = (x, lax.rem(x + 3, 4), lax.rem(x + 1, 4), lax.rem(x + 2, 4))
 
-    def o_copy(n, slot):
-        row = places[slot] * 4 + low
-        return copy_to(
-            ostage.at[n, slot], out_ref.at[row], o_send.at[n, slot], o_recv.at[n, slot], mates[n], head
+    def o_copy(n, slot, part, row_of=dp):
+        row = places[slot] * 4 + lax.rem(row_of, 4)
+        rows = pl.ds(0, FEAT) if n == 1 else pl.ds(part * PART, PART)
+        return copy_to(
+            ostage.at[n, slot, rows], out_ref.at[row, rows], o_send.at[n, slot, part], o_recv.at[n, slot, part],
+            mates[n], head,
         )
 
     def o_own(slot):
-        return pltpu.make_async_copy(ostage.at[0, slot], out_ref.at[places[slot] * 4 + low], o_send.at[0, slot])
-
-    def o_arrival(n, slot):
-        row = places[slot] * 4 + lax.rem(mates[n], 4)
-        return copy_to(
-            ostage.at[n, slot], out_ref.at[row], o_send.at[n, slot], o_recv.at[n, slot], mates[n], head
-        )
-
-    def emit(slots):
-        for n in (2, 3, 1, 0):
-            for at, slot in enumerate(slots):
-                ostage[n, slot] = total[n * FEAT : (n + 1) * FEAT, at * BLK : (at + 1) * BLK].astype(BF16)
-                if n:
-                    o_copy(n, slot).start()
-                else:
-                    o_own(slot).start()
-
-    for slots in ((0,), (1, 2), (3,)):
-        project(slots, len(slots) * BLK)
-        emit(slots)
+        return pltpu.make_async_copy(ostage.at[0, slot], out_ref.at[places[slot] * 4 + low], o_send.at[0, slot, 0])
+
+    def result(slot, row, count):
+        return total[row : row + count, slot * BLK : (slot + 1) * BLK].astype(BF16)
+
+    def emit_part(slots, part):
+        for slot in slots:
+            for n in (2, 3):
+                row = (FAR_B if part else FAR_A) + (n - 2) * PART
+                ostage[n, slot, part * PART : (part + 1) * PART] = result(slot, row, PART)
+                o_copy(n, slot, part).start()
+
+    def emit_chip(slots):
+        for slot in slots:
+            ostage[1, slot] = result(slot, MATE, FEAT)
+            o_copy(1, slot, 0).start()
+            ostage[0, slot] = result(slot, OWN, FEAT)
+            o_own(slot).start()
+
+    near, last = (0, 1, 2), (3,)
+    w_arrive(0)
+    project(near, FAR_A, FEAT)
+    emit_part(near, 0)
+    lax.fori_loop(RELAY, RELAY + CHUNKS, w_direct, 0)
+    emit_chip(near)
+    project(last, FAR_A, 3 * FEAT, 0, READY, arriving=True)
+    w_arrive(1)
+    project(near, FAR_B, FEAT)
+    emit_part(near, 1)
+    project(last, FAR_B, FEAT, 0, READY)
+    project(last, FAR_A, 4 * FEAT, READY, 8, arriving=True)
+    emit_part(last, 0)
+    emit_part(last, 1)
+    emit_chip(last)
 
     for slot in range(4):
-        for n in range(1, 4):
-            o_arrival(n, slot).wait_recv()
-            o_copy(n, slot).wait_send()
+        for n, part in ((1, 0), (2, 0), (3, 0), (2, 1), (3, 1)):
+            o_copy(n, slot, part, mates[n]).wait_recv()
+            o_copy(n, slot, part).wait_send()
         o_own(slot).wait()
 
     def sent(k, _):
@@ -317,11 +363,11 @@
         x_copy(0, k).wait_send()
         x_copy(1, k).wait_send()
         f_copy(k).wait_send()
-        s_copy(k).wait_send()
-        @pl.when(k < 8)
-        def _():
-            w_copy(k).wait_send()
-            z_copy(k, odd).wait_send()
+        pl.when(k < CHUNKS)(lambda: s_copy(k, 0).wait_send())
+        pl.when(k < CHUNKS)(lambda: s_copy(k, 1).wait_send())
+        pl.when(k < RELAY)(lambda: w_copy(k, 0).wait_send())
+        pl.when(jnp.logical_and(k >= RELAY, k < RELAY + CHUNKS))(lambda: w_copy(k, 1).wait_send())
+        pl.when(k < RELAY)(lambda: z_copy(k, odd).wait_send())
         return 0
 
     lax.fori_loop(0, HEADS, sent, 0)
@@ -345,17 +391,17 @@
             pltpu.VMEM((HEADS, BLK, 256), BF16),
             pltpu.VMEM((4, HEADS, BLK, 256), BF16),
             pltpu.VMEM((HEADS, 4 * FEAT, 256), BF16),
-            pltpu.VMEM((4 * FEAT, 2 * BLK), F32),
+            pltpu.VMEM((4 * FEAT, 4 * BLK), F32),
             pltpu.VMEM((4, 4, FEAT, BLK), BF16),
             dma((3,)), dma((HEADS,)),
             dma((HEADS,)), dma((HEADS,)),
             dma((2, HEADS)), dma((2, HEADS)),
             dma((HEADS,)), dma((HEADS,)),
-            dma((8,)), dma((8,)),
-            dma((8,)), dma((8,)),
-            dma((HEADS,)), dma((HEADS,)),
+            dma((RELAY + CHUNKS,)), dma((RELAY + CHUNKS,)),
+            dma((RELAY,)), dma((RELAY,)),
+            dma((2, CHUNKS)), dma((2, CHUNKS)),
             dma, dma,
-            dma((4, 4)), dma((4, 4)),
+            dma((4, 4, 2)), dma((4, 4, 2)),
         ],
         compiler_params=pltpu.CompilerParams(
             collective_id=0, has_side_effects=True, vmem_limit_bytes=56 * 1024 * 1024

time: 75.7 us -> 70.6 us (0.933)
  Pallas kernels: 73.1 us -> 68.1 us
    pallas_call x1, Pallas kernels: 73.1 us -> 68.1 us  [body(): pl.pallas_call(kernel, out_shape=jax.ShapeDtypeStruct((16, FEAT, BLK), BF...]
where the time goes in v3:
time: 70.6 us; the launch traced here: 70.5 us
  Pallas kernels  68.1 us (96%)
  local copies, waits for them, and re-layouts  2.36 us (3%)
    pallas_call x1, Pallas kernels, body(): pl.pallas_call(kernel, out_shape=jax.ShapeDtypeStruct((16, FEAT, BLK), BF...  68.1 us
    unnamed x1, local copies, waits for them, and re-layouts  2.36 us

profile of v3, /device:TPU:1, one launch (start us, length us, event | category | flops | bytes accessed | tf_op | source)
XLA Modules:
  0.0 70.5 jit_solution(16266893143701841043)
XLA Ops:
  0.0 68.1 %shard_map.55 = bf16[16,288,128]{2,1,0:T(8,128)(2,1)} custom-call(bf16[2048,256]{1,0:T(8,128)(2,1)} %q_hbm.1, bf16[2048,128]{1,0:T(8,128)(2,1)} %k_hbm.1, bf16[2048,128]{1,0:T(8,128)(2,1)} %v_hbm.1, s32[16,16]{1,0:T(8,128)} %doc_ref.1, bf16[288,4096]{1,0:T(8,128)(2,1)} %bitcast.3), custom_call_target="tpu_custom_call" | custom-call | tf_op jit(solution)/shard_map/pallas_call | solution.py:380
  68.1 2.4 %copy.7 = bf16[16,128,288]{1,2,0:T(8,128)(2,1)} copy(bf16[16,128,288]{1,2,0:T(8,128)(2,1)} %bitcast.2) | data formatting | bytes 2359296

commit v4 on v3

--- a/solution.py
+++ b/solution.py
@@ -19,7 +19,7 @@
 RELAY = 4
 CHUNKS = 8
 FAR_A, BOTH_A, OWN, MATE, FAR_B, BOTH_B = 0, PART, FEAT, 2 * FEAT, 3 * FEAT, 3 * FEAT + PART
-LAG_A, LAG_W, LAG_Z, LAG_X = 5, 15, 20, 14
+LAG_A, LAG_W, LAG_Z, LAG_X = 5, 16, 23, 14
 SCALE = 1.0 / 12.0 / 50.0
 GAIN = 50.0 * math.log2(math.e)
 MESH = pl.DeviceIdType.MESH
@@ -140,8 +140,8 @@
                 both = both + tile(q_two, block, n, False)
             acc[...] = both
 
-        pl.when(block < 8)(lambda: tiles(3))
-        pl.when(block >= 8)(lambda: tiles(7))
+        for level in range(4):
+            pl.when(block // 4 == level)(lambda: tiles(2 * level + 1))
         both = acc[...]
         result = (both[:, 0:HD] / both[:, HD : 2 * HD]).astype(BF16)
         into[...] = jnp.concatenate([result[0:BLK], result[BLK : 2 * BLK]], axis=1)
@@ -214,6 +214,8 @@
         return 0
 
     lax.fori_loop(1, EARLY, early_send, 0)
+    x_copy(0, 0).start()
+    x_copy(1, 0).start()
 
     def send_w(n, _):
         w_copy(n, 0).start()
@@ -236,8 +238,10 @@
             @pl.when(k > 0)
             def _():
                 a_copy(k).wait_recv()
-            x_copy(0, k).start()
-            x_copy(1, k).start()
+            @pl.when(k > 0)
+            def _():
+                x_copy(0, k).start()
+                x_copy(1, k).start()
 
         def pass_w(n):
             w_copy(n, 0).wait_recv()

time: 70.6 us -> 70 us (level)
  no operation moved by 1% of the time
where the time goes in v4:
time: 70 us; the launch traced here: 69.8 us
  Pallas kernels  67.4 us (96%)
  local copies, waits for them, and re-layouts  2.36 us (3%)
    pallas_call x1, Pallas kernels, body(): pl.pallas_call(kernel, out_shape=jax.ShapeDtypeStruct((16, FEAT, BLK), BF...  67.4 us
    unnamed x1, local copies, waits for them, and re-layouts  2.36 us

profile of v4, /device:TPU:1, one launch (start us, length us, event | category | flops | bytes accessed | tf_op | source)
XLA Modules:
  0.0 69.8 jit_solution(9906462251160464300)
XLA Ops:
  0.0 67.4 %shard_map.55 = bf16[16,288,128]{2,1,0:T(8,128)(2,1)} custom-call(bf16[2048,256]{1,0:T(8,128)(2,1)} %q_hbm.1, bf16[2048,128]{1,0:T(8,128)(2,1)} %k_hbm.1, bf16[2048,128]{1,0:T(8,128)(2,1)} %v_hbm.1, s32[16,16]{1,0:T(8,128)} %doc_ref.1, bf16[288,4096]{1,0:T(8,128)(2,1)} %bitcast.3), custom_call_target="tpu_custom_call" | custom-call | tf_op jit(solution)/shard_map/pallas_call | solution.py:384
  67.4 2.4 %copy.7 = bf16[16,128,288]{1,2,0:T(8,128)(2,1)} copy(bf16[16,128,288]{1,2,0:T(8,128)(2,1)} %bitcast.2) | data formatting | bytes 2359296
